TPU v7x, 32 devices: a whole 2x2x4 slice. The times are simulated.
32 devices in a mesh: lev: 2 (over x), gx: 8 (over z, y), gy: 2 (over core).
Axes of the slice: x: 2, y: 2, z: 4, core: 2. Of those that a mesh axis runs over, the one named last changes fastest.
Arguments:
- increments: float32 [1, 2, 80, 128, 256], P(None, None, 'lev', 'gx', 'gy'), may hold values from -6 to 6
- vert_corr: float32 [2, 80, 80], replicated, may hold values from -0.025 to 1, as said below
- kappa: float32 [2, 128, 256], P(None, 'gx', 'gy'), may hold values from 0.03 to 0.24
- sea_mask: int32 [80, 128, 256], P('lev', 'gx', 'gy'), may hold values 0 or 1
- level_count: int32 [128, 256], P('gx', 'gy'), may hold values from 10 to 75
Outputs:
- covaried: float32 [1, 2, 80, 128, 256], P(None, None, 'lev', 'gx', 'gy')
Inputs may be any that keep to these rules, and one draw needn't show every extreme that they name: vert_corr has ones on the diagonal, and each row's other entries together have magnitude below one.
All inputs are finite; a program needn't handle non-finite values. No bound on the sum of `sea_mask` on one device may be relied on, other than what follows from the above.
Results may differ from a plain program's by a relative error of at most 0.00021.
Values sent between devices are 32-bit elements; how exact they have to be, the bound alone decides.
A program may use at most 64 MiB of HBM per device.

v0:
```python
import jax
import jax.numpy as jnp
from jax import lax
from jax.sharding import PartitionSpec as P

PASSES = 10


def from_behind(block, axis, distance):
    devices = range(lax.axis_size(axis))
    route = [((i - distance) % len(devices), i) for i in devices]
    return lax.ppermute(block, axis, route)


def shifted(block, axis, distance):
    devices = range(lax.axis_size(axis))
    route = [(i - distance, i) for i in devices if i - distance in devices]
    return lax.ppermute(block, axis, route)


def padded(cells, sides, width):
    for axis, dim in sides:
        count = lax.axis_size(axis)
        head = lax.slice_in_dim(cells, 0, width, axis=dim)
        tail = lax.slice_in_dim(cells, cells.shape[dim] - width, cells.shape[dim], axis=dim)
        cells = jnp.concatenate(
            [
                lax.ppermute(tail, axis, [(i, (i + 1) % count) for i in range(count)]),
                cells,
                lax.ppermute(head, axis, [((i + 1) % count, i) for i in range(count)]),
            ],
            axis=dim,
        )
    return cells


def relax(extended, east_ext, north_ext, wet_center):
    center = extended[..., 1:-1, 1:-1]
    flux = east_ext[1:-1, 1:-1] * (extended[..., 2:, 1:-1] - center)
    flux = flux + east_ext[:-2, 1:-1] * (extended[..., :-2, 1:-1] - center)
    flux = flux + north_ext[1:-1, 1:-1] * (extended[..., 1:-1, 2:] - center)
    flux = flux + north_ext[1:-1, :-2] * (extended[..., 1:-1, :-2] - center)
    return wet_center * (center + flux)


def per_device(increments, vert_corr, kappa, sea_mask, level_count):
    lev_dev = sea_mask.shape[0]
    cells_x = sea_mask.shape[1]
    cells_y = sea_mask.shape[2]
    lev_first = lax.axis_index("lev") * lev_dev
    levels = lev_first + jnp.arange(lev_dev, dtype=jnp.int32)
    wet = sea_mask * (levels[:, None, None] < level_count[None]).astype(jnp.int32)
    wet_float = wet.astype(jnp.float32)
    masked = increments * wet_float
    own_rows = lax.dynamic_slice_in_dim(vert_corr, lev_first, lev_dev, 1)
    correlated = jnp.einsum(
        "toh,dthxy->dtoxy",
        own_rows,
        lax.all_gather(masked, "lev", axis=2, tiled=True),
        precision=lax.Precision.HIGHEST,
    )
    field = correlated * wet_float
    total_y = cells_y * lax.axis_size("gy")
    local_rows = lax.axis_index("gy") * cells_y + jnp.arange(cells_y, dtype=jnp.int32)
    open_local = (local_rows != total_y - 1).astype(jnp.float32)
    east_local = kappa[0]
    north_local = kappa[1] * open_local[None, :]
    east_low = from_behind(east_local[-1:, :], "gx", 1)
    north_low = shifted(north_local[:, -1:], "gy", 1)
    zero_row = jnp.zeros((1, cells_y), jnp.float32)
    zero_col = jnp.zeros((cells_x, 1), jnp.float32)
    east_ext = jnp.pad(jnp.concatenate([east_low, east_local, zero_row], axis=0), ((0, 0), (1, 1)))
    north_ext = jnp.pad(
        jnp.concatenate([north_low, north_local, zero_col], axis=1), ((1, 1), (0, 0))
    )

    def one_pass(step, current):
        extended = padded(current, (("gx", 3), ("gy", 4)), 1)
        return relax(extended, east_ext, north_ext, wet_float)

    field = lax.fori_loop(0, PASSES, one_pass, field)
    return field


def solution(mesh):
    in_specs = (
        P(None, None, "lev", "gx", "gy"),
        P(),
        P(None, "gx", "gy"),
        P("lev", "gx", "gy"),
        P("gx", "gy"),
    )
    out_specs = P(None, None, "lev", "gx", "gy")
    return jax.shard_map(
        per_device, mesh=mesh, in_specs=in_specs, out_specs=out_specs, check_vma=False
    )
```

profile of v0, /device:TPU:0, one launch (start us, length us, event | category | flops | bytes accessed | tf_op | source)
XLA Modules:
  0.0 171.8 jit_solution(11940098655885477659)
XLA Ops:
  7.7 2.1 %copy_multiply_fusion = f32[1,2,40,16,128]{4,2,3,1,0:T(8,128)} fusion(f32[1,2,40,16,128]{4,3,2,1,0:T(8,128)} %param.7, f32[40,16,128]{2,0,1:T(8,128)S(1)} %fusion.21), kind=kLoop, calls=%fused_computation.24 | loop fusion | flops 163840 | bytes 1638400 | tf_op jit(solution)/shard_map/mul | solution.py:54
  9.9 3.0 %collective-permute-start.4 = (f32[1,128]{1,0:T(1,128)S(1)}, f32[1,128]{1,0:T(1,128)S(1)}, u32[]{:S(2)}, u32[]{:S(2)}) collective-permute-start(f32[1,128]{1,0:T(1,128)S(1)} %slice_bitcast_fusion.1), channel_id=1, source_target_pairs={{14,0},{0,2},{2,4},{4,6},{6,8},{8,10},{10,12},{12,14},{15,1},{1,3}... | collective-permute-start | bytes 1544 | tf_op jit(solution)/shard_map/ppermute | solution.py:12
  15.3 2.1 %collective-permute-done.4 = f32[1,128]{1,0:T(1,128)S(1)} collective-permute-done((f32[1,128]{1,0:T(1,128)S(1)}, f32[1,128]{1,0:T(1,128)S(1)}, u32[]{:S(2)}, u32[]{:S(2)}) %collective-permute-start.4) | collective-permute-done | bytes 544 | tf_op jit(solution)/shard_map/ppermute | solution.py:12
  17.6 19.4 %all-gather.2.cloned.1.call-done = f32[1,2,80,16,128]{4,2,3,1,0:T(8,128)} async-done(((f32[1,2,40,16,128]{4,2,3,1,0:T(8,128)}), f32[1,2,80,16,128]{4,2,3,1,0:T(8,128)}) %all-gather.2.cloned.1.call-update) | async-done | bytes 1310736 | tf_op jit(solution)/shard_map/all_gather | solution.py:59
  37.0 3.0 %fusion.18 = f32[1,2,40,16,128]{4,2,3,1,0:T(8,128)} fusion(f32[1,2,80,16,128]{4,2,3,1,0:T(8,128)} %all-gather.2.cloned.1.call-done, f32[40,16,128]{2,0,1:T(8,128)S(1)} %fusion.21, f32[2,80,80]{2,1,0:T(8,128)S(1)} %copy-done, s32[]{:T(128)S(6)} %select_n.3), kind=kOutput, calls=%fused_computation.23 | convolution fusion | flops 157450240 | bytes 2334724 | tf_op jit(solution)/shard_map/toh,dthxy->dtoxy/dot_general | solution.py:56
  40.0 122.9 %while.10 = (s32[]{:T(128)}, f32[1,2,40,16,128]{4,2,3,1,0:T(8,128)}, f32[40,16,128]{2,0,1:T(8,128)S(1)}, f32[18,130]{1,0:T(8,128)S(1)}, f32[18,130]{1,0:T(8,128)S(1)}, /*index=5*/s32[]{:T(128)}) while((s32[]{:T(128)}, f32[1,2,40,16,128]{4,2,3,1,0:T(8,128)}, f32[40,16,128]{2,0,1:T(8,128)S(1)}, f32[18,130]{1,0:T(8,128)S(1)}, ...), condition=%wide.region_1.2_spmd, body=%wide.region_0.1_spmd.sunk | while | flops 2785282 | bytes 5959653 | solution.py:81
  41.1 1.5 collective-permute-start
  42.6 3.2 %collective-permute-start.1 = (f32[1,2,40,1,128]{4,2,3,1,0:T(8,128)S(1)}, f32[1,2,40,1,128]{4,2,3,1,0:T(8,128)S(1)}, u32[]{:S(2)}, u32[]{:S(2)}) collective-permute-start(f32[1,2,40,1,128]{4,2,3,1,0:T(8,128)S(1)} %get-tuple-element.103), channel_id=1, source_target_pairs={{2,0},{4,2},{6,4},{8,6},{10,8},{12,10},{14,12},{0,14},{3,1},{5,3},... | collective-permute-start | bytes 122888 | tf_op jit(solution)/shard_map/while/body/eval_jaxpr/ppermute | solution.py:30
  45.8 2.0 %collective-permute-done = f32[1,2,40,1,128]{4,2,3,1,0:T(8,128)S(1)} collective-permute-done((f32[1,2,40,1,128]{4,2,3,1,0:T(8,128)S(1)}, f32[1,2,40,1,128]{4,2,3,1,0:T(8,128)S(1)}, u32[]{:S(2)}, u32[]{:S(2)}) %collective-permute-start) | collective-permute-done | bytes 40992 | tf_op jit(solution)/shard_map/while/body/eval_jaxpr/ppermute | solution.py:28
  50.8 1.5 fusion.36
  54.5 3.6 %collective-permute-start.1 = (f32[1,2,40,1,128]{4,2,3,1,0:T(8,128)S(1)}, f32[1,2,40,1,128]{4,2,3,1,0:T(8,128)S(1)}, u32[]{:S(2)}, u32[]{:S(2)}) collective-permute-start(f32[1,2,40,1,128]{4,2,3,1,0:T(8,128)S(1)} %get-tuple-element.103), channel_id=1, source_target_pairs={{2,0},{4,2},{6,4},{8,6},{10,8},{12,10},{14,12},{0,14},{3,1},{5,3},... | collective-permute-start | bytes 122888 | tf_op jit(solution)/shard_map/while/body/eval_jaxpr/ppermute | solution.py:30
  58.1 2.0 %collective-permute-done = f32[1,2,40,1,128]{4,2,3,1,0:T(8,128)S(1)} collective-permute-done((f32[1,2,40,1,128]{4,2,3,1,0:T(8,128)S(1)}, f32[1,2,40,1,128]{4,2,3,1,0:T(8,128)S(1)}, u32[]{:S(2)}, u32[]{:S(2)}) %collective-permute-start) | collective-permute-done | bytes 40992 | tf_op jit(solution)/shard_map/while/body/eval_jaxpr/ppermute | solution.py:28
  65.7 4.7 %collective-permute-start.1 = (f32[1,2,40,1,128]{4,2,3,1,0:T(8,128)S(1)}, f32[1,2,40,1,128]{4,2,3,1,0:T(8,128)S(1)}, u32[]{:S(2)}, u32[]{:S(2)}) collective-permute-start(f32[1,2,40,1,128]{4,2,3,1,0:T(8,128)S(1)} %get-tuple-element.103), channel_id=1, source_target_pairs={{2,0},{4,2},{6,4},{8,6},{10,8},{12,10},{14,12},{0,14},{3,1},{5,3},... | collective-permute-start | bytes 122888 | tf_op jit(solution)/shard_map/while/body/eval_jaxpr/ppermute | solution.py:30
  70.4 2.0 %collective-permute-done = f32[1,2,40,1,128]{4,2,3,1,0:T(8,128)S(1)} collective-permute-done((f32[1,2,40,1,128]{4,2,3,1,0:T(8,128)S(1)}, f32[1,2,40,1,128]{4,2,3,1,0:T(8,128)S(1)}, u32[]{:S(2)}, u32[]{:S(2)}) %collective-permute-start) | collective-permute-done | bytes 40992 | tf_op jit(solution)/shard_map/while/body/eval_jaxpr/ppermute | solution.py:28
  77.9 4.7 %collective-permute-start.1 = (f32[1,2,40,1,128]{4,2,3,1,0:T(8,128)S(1)}, f32[1,2,40,1,128]{4,2,3,1,0:T(8,128)S(1)}, u32[]{:S(2)}, u32[]{:S(2)}) collective-permute-start(f32[1,2,40,1,128]{4,2,3,1,0:T(8,128)S(1)} %get-tuple-element.103), channel_id=1, source_target_pairs={{2,0},{4,2},{6,4},{8,6},{10,8},{12,10},{14,12},{0,14},{3,1},{5,3},... | collective-permute-start | bytes 122888 | tf_op jit(solution)/shard_map/while/body/eval_jaxpr/ppermute | solution.py:30
  82.6 2.0 %collective-permute-done = f32[1,2,40,1,128]{4,2,3,1,0:T(8,128)S(1)} collective-permute-done((f32[1,2,40,1,128]{4,2,3,1,0:T(8,128)S(1)}, f32[1,2,40,1,128]{4,2,3,1,0:T(8,128)S(1)}, u32[]{:S(2)}, u32[]{:S(2)}) %collective-permute-start) | collective-permute-done | bytes 40992 | tf_op jit(solution)/shard_map/while/body/eval_jaxpr/ppermute | solution.py:28
  87.7 1.5 fusion.36
  90.2 4.7 %collective-permute-start.1 = (f32[1,2,40,1,128]{4,2,3,1,0:T(8,128)S(1)}, f32[1,2,40,1,128]{4,2,3,1,0:T(8,128)S(1)}, u32[]{:S(2)}, u32[]{:S(2)}) collective-permute-start(f32[1,2,40,1,128]{4,2,3,1,0:T(8,128)S(1)} %get-tuple-element.103), channel_id=1, source_target_pairs={{2,0},{4,2},{6,4},{8,6},{10,8},{12,10},{14,12},{0,14},{3,1},{5,3},... | collective-permute-start | bytes 122888 | tf_op jit(solution)/shard_map/while/body/eval_jaxpr/ppermute | solution.py:30
  95.0 2.0 %collective-permute-done = f32[1,2,40,1,128]{4,2,3,1,0:T(8,128)S(1)} collective-permute-done((f32[1,2,40,1,128]{4,2,3,1,0:T(8,128)S(1)}, f32[1,2,40,1,128]{4,2,3,1,0:T(8,128)S(1)}, u32[]{:S(2)}, u32[]{:S(2)}) %collective-permute-start) | collective-permute-done | bytes 40992 | tf_op jit(solution)/shard_map/while/body/eval_jaxpr/ppermute | solution.py:28
  100.0 1.5 fusion.36
  102.5 4.7 %collective-permute-start.1 = (f32[1,2,40,1,128]{4,2,3,1,0:T(8,128)S(1)}, f32[1,2,40,1,128]{4,2,3,1,0:T(8,128)S(1)}, u32[]{:S(2)}, u32[]{:S(2)}) collective-permute-start(f32[1,2,40,1,128]{4,2,3,1,0:T(8,128)S(1)} %get-tuple-element.103), channel_id=1, source_target_pairs={{2,0},{4,2},{6,4},{8,6},{10,8},{12,10},{14,12},{0,14},{3,1},{5,3},... | collective-permute-start | bytes 122888 | tf_op jit(solution)/shard_map/while/body/eval_jaxpr/ppermute | solution.py:30
  107.2 2.0 %collective-permute-done = f32[1,2,40,1,128]{4,2,3,1,0:T(8,128)S(1)} collective-permute-done((f32[1,2,40,1,128]{4,2,3,1,0:T(8,128)S(1)}, f32[1,2,40,1,128]{4,2,3,1,0:T(8,128)S(1)}, u32[]{:S(2)}, u32[]{:S(2)}) %collective-permute-start) | collective-permute-done | bytes 40992 | tf_op jit(solution)/shard_map/while/body/eval_jaxpr/ppermute | solution.py:28
  114.8 4.7 %collective-permute-start.1 = (f32[1,2,40,1,128]{4,2,3,1,0:T(8,128)S(1)}, f32[1,2,40,1,128]{4,2,3,1,0:T(8,128)S(1)}, u32[]{:S(2)}, u32[]{:S(2)}) collective-permute-start(f32[1,2,40,1,128]{4,2,3,1,0:T(8,128)S(1)} %get-tuple-element.103), channel_id=1, source_target_pairs={{2,0},{4,2},{6,4},{8,6},{10,8},{12,10},{14,12},{0,14},{3,1},{5,3},... | collective-permute-start | bytes 122888 | tf_op jit(solution)/shard_map/while/body/eval_jaxpr/ppermute | solution.py:30
  119.5 2.0 %collective-permute-done = f32[1,2,40,1,128]{4,2,3,1,0:T(8,128)S(1)} collective-permute-done((f32[1,2,40,1,128]{4,2,3,1,0:T(8,128)S(1)}, f32[1,2,40,1,128]{4,2,3,1,0:T(8,128)S(1)}, u32[]{:S(2)}, u32[]{:S(2)}) %collective-permute-start) | collective-permute-done | bytes 40992 | tf_op jit(solution)/shard_map/while/body/eval_jaxpr/ppermute | solution.py:28
  127.1 4.7 %collective-permute-start.1 = (f32[1,2,40,1,128]{4,2,3,1,0:T(8,128)S(1)}, f32[1,2,40,1,128]{4,2,3,1,0:T(8,128)S(1)}, u32[]{:S(2)}, u32[]{:S(2)}) collective-permute-start(f32[1,2,40,1,128]{4,2,3,1,0:T(8,128)S(1)} %get-tuple-element.103), channel_id=1, source_target_pairs={{2,0},{4,2},{6,4},{8,6},{10,8},{12,10},{14,12},{0,14},{3,1},{5,3},... | collective-permute-start | bytes 122888 | tf_op jit(solution)/shard_map/while/body/eval_jaxpr/ppermute | solution.py:30
  131.8 2.0 %collective-permute-done = f32[1,2,40,1,128]{4,2,3,1,0:T(8,128)S(1)} collective-permute-done((f32[1,2,40,1,128]{4,2,3,1,0:T(8,128)S(1)}, f32[1,2,40,1,128]{4,2,3,1,0:T(8,128)S(1)}, u32[]{:S(2)}, u32[]{:S(2)}) %collective-permute-start) | collective-permute-done | bytes 40992 | tf_op jit(solution)/shard_map/while/body/eval_jaxpr/ppermute | solution.py:28
  136.9 1.5 fusion.36
  139.4 4.7 %collective-permute-start.1 = (f32[1,2,40,1,128]{4,2,3,1,0:T(8,128)S(1)}, f32[1,2,40,1,128]{4,2,3,1,0:T(8,128)S(1)}, u32[]{:S(2)}, u32[]{:S(2)}) collective-permute-start(f32[1,2,40,1,128]{4,2,3,1,0:T(8,128)S(1)} %get-tuple-element.103), channel_id=1, source_target_pairs={{2,0},{4,2},{6,4},{8,6},{10,8},{12,10},{14,12},{0,14},{3,1},{5,3},... | collective-permute-start | bytes 122888 | tf_op jit(solution)/shard_map/while/body/eval_jaxpr/ppermute | solution.py:30
  144.1 2.0 %collective-permute-done = f32[1,2,40,1,128]{4,2,3,1,0:T(8,128)S(1)} collective-permute-done((f32[1,2,40,1,128]{4,2,3,1,0:T(8,128)S(1)}, f32[1,2,40,1,128]{4,2,3,1,0:T(8,128)S(1)}, u32[]{:S(2)}, u32[]{:S(2)}) %collective-permute-start) | collective-permute-done | bytes 40992 | tf_op jit(solution)/shard_map/while/body/eval_jaxpr/ppermute | solution.py:28
  151.7 4.7 %collective-permute-start.1 = (f32[1,2,40,1,128]{4,2,3,1,0:T(8,128)S(1)}, f32[1,2,40,1,128]{4,2,3,1,0:T(8,128)S(1)}, u32[]{:S(2)}, u32[]{:S(2)}) collective-permute-start(f32[1,2,40,1,128]{4,2,3,1,0:T(8,128)S(1)} %get-tuple-element.103), channel_id=1, source_target_pairs={{2,0},{4,2},{6,4},{8,6},{10,8},{12,10},{14,12},{0,14},{3,1},{5,3},... | collective-permute-start | bytes 122888 | tf_op jit(solution)/shard_map/while/body/eval_jaxpr/ppermute | solution.py:30
  156.4 2.0 %collective-permute-done = f32[1,2,40,1,128]{4,2,3,1,0:T(8,128)S(1)} collective-permute-done((f32[1,2,40,1,128]{4,2,3,1,0:T(8,128)S(1)}, f32[1,2,40,1,128]{4,2,3,1,0:T(8,128)S(1)}, u32[]{:S(2)}, u32[]{:S(2)}) %collective-permute-start) | collective-permute-done | bytes 40992 | tf_op jit(solution)/shard_map/while/body/eval_jaxpr/ppermute | solution.py:28
  162.9 2.0 %copy.20 = f32[1,2,40,16,128]{4,3,2,1,0:T(8,128)} copy(f32[1,2,40,16,128]{4,2,3,1,0:T(8,128)} %get-tuple-element.32) | data formatting | bytes 1310720 | tf_op jit(solution)/shard_map/while | solution.py:81
  (196 shorter events, 54.5 us)
Async XLA Ops:
  6.5 30.4 %all-gather.2.cloned.1.call-start = ((), (), s32[]{:S(2)}) async-start(), calls=%async_computation | async-start | bytes 1966080 | tf_op jit(solution)/shard_map/all_gather | solution.py:59
  9.9 7.6 %collective-permute-start.4 = (f32[1,128]{1,0:T(1,128)S(1)}, f32[1,128]{1,0:T(1,128)S(1)}, u32[]{:S(2)}, u32[]{:S(2)}) collective-permute-start(f32[1,128]{1,0:T(1,128)S(1)} %slice_bitcast_fusion.1), channel_id=1, source_target_pairs={{14,0},{0,2},{2,4},{4,6},{6,8},{8,10},{10,12},{12,14},{15,1},{1,3}... | collective-permute-start | bytes 1544 | tf_op jit(solution)/shard_map/ppermute | solution.py:12
  13.0 2.3 %collective-permute-start.5 = (f32[16,1]{1,0:T(8,128)S(1)}, f32[16,1]{1,0:T(8,128)S(1)}, u32[]{:S(2)}, u32[]{:S(2)}) collective-permute-start(f32[16,1]{1,0:T(8,128)S(1)} %slice.63), channel_id=1, source_target_pairs={{0,1},{2,3},{4,5},{6,7},{8,9},{10,11},{12,13},{14,15},{16,17},{18,... | collective-permute-start | bytes 200 | tf_op jit(solution)/shard_map/ppermute | solution.py:18
  41.1 6.7 %collective-permute-start = (f32[1,2,40,1,128]{4,2,3,1,0:T(8,128)S(1)}, f32[1,2,40,1,128]{4,2,3,1,0:T(8,128)S(1)}, u32[]{:S(2)}, u32[]{:S(2)}) collective-permute-start(f32[1,2,40,1,128]{4,2,3,1,0:T(8,128)S(1)} %get-tuple-element.102), channel_id=1, source_target_pairs={{0,2},{2,4},{4,6},{6,8},{8,10},{10,12},{12,14},{14,0},{1,3},{3,5},... | collective-permute-start | bytes 122888 | tf_op jit(solution)/shard_map/while/body/eval_jaxpr/ppermute | solution.py:28
  42.6 5.2 %collective-permute-start.1 = (f32[1,2,40,1,128]{4,2,3,1,0:T(8,128)S(1)}, f32[1,2,40,1,128]{4,2,3,1,0:T(8,128)S(1)}, u32[]{:S(2)}, u32[]{:S(2)}) collective-permute-start(f32[1,2,40,1,128]{4,2,3,1,0:T(8,128)S(1)} %get-tuple-element.103), channel_id=1, source_target_pairs={{2,0},{4,2},{6,4},{8,6},{10,8},{12,10},{14,12},{0,14},{3,1},{5,3},... | collective-permute-start | bytes 122888 | tf_op jit(solution)/shard_map/while/body/eval_jaxpr/ppermute | solution.py:30
  48.7 1.8 %collective-permute-start.3 = (f32[1,2,40,18,1]{2,1,4,3,0:T(2,128)S(1)}, f32[1,2,40,18,1]{2,1,4,3,0:T(2,128)S(1)}, u32[]{:S(2)}, u32[]{:S(2)}) collective-permute-start(f32[1,2,40,18,1]{2,1,4,3,0:T(2,128)S(1)} %copy.34), channel_id=1, source_target_pairs={{1,0},{0,1},{3,2},{2,3},{5,4},{4,5},{7,6},{6,7},{9,8},{8,9},{11,10... | collective-permute-start | bytes 17288 | tf_op jit(solution)/shard_map/while/body/eval_jaxpr/ppermute | solution.py:30
  53.3 6.7 %collective-permute-start = (f32[1,2,40,1,128]{4,2,3,1,0:T(8,128)S(1)}, f32[1,2,40,1,128]{4,2,3,1,0:T(8,128)S(1)}, u32[]{:S(2)}, u32[]{:S(2)}) collective-permute-start(f32[1,2,40,1,128]{4,2,3,1,0:T(8,128)S(1)} %get-tuple-element.102), channel_id=1, source_target_pairs={{0,2},{2,4},{4,6},{6,8},{8,10},{10,12},{12,14},{14,0},{1,3},{3,5},... | collective-permute-start | bytes 122888 | tf_op jit(solution)/shard_map/while/body/eval_jaxpr/ppermute | solution.py:28
  54.5 5.7 %collective-permute-start.1 = (f32[1,2,40,1,128]{4,2,3,1,0:T(8,128)S(1)}, f32[1,2,40,1,128]{4,2,3,1,0:T(8,128)S(1)}, u32[]{:S(2)}, u32[]{:S(2)}) collective-permute-start(f32[1,2,40,1,128]{4,2,3,1,0:T(8,128)S(1)} %get-tuple-element.103), channel_id=1, source_target_pairs={{2,0},{4,2},{6,4},{8,6},{10,8},{12,10},{14,12},{0,14},{3,1},{5,3},... | collective-permute-start | bytes 122888 | tf_op jit(solution)/shard_map/while/body/eval_jaxpr/ppermute | solution.py:30
  61.0 1.8 %collective-permute-start.3 = (f32[1,2,40,18,1]{2,1,4,3,0:T(2,128)S(1)}, f32[1,2,40,18,1]{2,1,4,3,0:T(2,128)S(1)}, u32[]{:S(2)}, u32[]{:S(2)}) collective-permute-start(f32[1,2,40,18,1]{2,1,4,3,0:T(2,128)S(1)} %copy.34), channel_id=1, source_target_pairs={{1,0},{0,1},{3,2},{2,3},{5,4},{4,5},{7,6},{6,7},{9,8},{8,9},{11,10... | collective-permute-start | bytes 17288 | tf_op jit(solution)/shard_map/while/body/eval_jaxpr/ppermute | solution.py:30
  65.6 6.7 %collective-permute-start = (f32[1,2,40,1,128]{4,2,3,1,0:T(8,128)S(1)}, f32[1,2,40,1,128]{4,2,3,1,0:T(8,128)S(1)}, u32[]{:S(2)}, u32[]{:S(2)}) collective-permute-start(f32[1,2,40,1,128]{4,2,3,1,0:T(8,128)S(1)} %get-tuple-element.102), channel_id=1, source_target_pairs={{0,2},{2,4},{4,6},{6,8},{8,10},{10,12},{12,14},{14,0},{1,3},{3,5},... | collective-permute-start | bytes 122888 | tf_op jit(solution)/shard_map/while/body/eval_jaxpr/ppermute | solution.py:28
  65.7 6.7 %collective-permute-start.1 = (f32[1,2,40,1,128]{4,2,3,1,0:T(8,128)S(1)}, f32[1,2,40,1,128]{4,2,3,1,0:T(8,128)S(1)}, u32[]{:S(2)}, u32[]{:S(2)}) collective-permute-start(f32[1,2,40,1,128]{4,2,3,1,0:T(8,128)S(1)} %get-tuple-element.103), channel_id=1, source_target_pairs={{2,0},{4,2},{6,4},{8,6},{10,8},{12,10},{14,12},{0,14},{3,1},{5,3},... | collective-permute-start | bytes 122888 | tf_op jit(solution)/shard_map/while/body/eval_jaxpr/ppermute | solution.py:30
  73.3 1.8 %collective-permute-start.3 = (f32[1,2,40,18,1]{2,1,4,3,0:T(2,128)S(1)}, f32[1,2,40,18,1]{2,1,4,3,0:T(2,128)S(1)}, u32[]{:S(2)}, u32[]{:S(2)}) collective-permute-start(f32[1,2,40,18,1]{2,1,4,3,0:T(2,128)S(1)} %copy.34), channel_id=1, source_target_pairs={{1,0},{0,1},{3,2},{2,3},{5,4},{4,5},{7,6},{6,7},{9,8},{8,9},{11,10... | collective-permute-start | bytes 17288 | tf_op jit(solution)/shard_map/while/body/eval_jaxpr/ppermute | solution.py:30
  77.9 6.7 %collective-permute-start = (f32[1,2,40,1,128]{4,2,3,1,0:T(8,128)S(1)}, f32[1,2,40,1,128]{4,2,3,1,0:T(8,128)S(1)}, u32[]{:S(2)}, u32[]{:S(2)}) collective-permute-start(f32[1,2,40,1,128]{4,2,3,1,0:T(8,128)S(1)} %get-tuple-element.102), channel_id=1, source_target_pairs={{0,2},{2,4},{4,6},{6,8},{8,10},{10,12},{12,14},{14,0},{1,3},{3,5},... | collective-permute-start | bytes 122888 | tf_op jit(solution)/shard_map/while/body/eval_jaxpr/ppermute | solution.py:28
  77.9 6.8 %collective-permute-start.1 = (f32[1,2,40,1,128]{4,2,3,1,0:T(8,128)S(1)}, f32[1,2,40,1,128]{4,2,3,1,0:T(8,128)S(1)}, u32[]{:S(2)}, u32[]{:S(2)}) collective-permute-start(f32[1,2,40,1,128]{4,2,3,1,0:T(8,128)S(1)} %get-tuple-element.103), channel_id=1, source_target_pairs={{2,0},{4,2},{6,4},{8,6},{10,8},{12,10},{14,12},{0,14},{3,1},{5,3},... | collective-permute-start | bytes 122888 | tf_op jit(solution)/shard_map/while/body/eval_jaxpr/ppermute | solution.py:30
  85.6 1.8 %collective-permute-start.3 = (f32[1,2,40,18,1]{2,1,4,3,0:T(2,128)S(1)}, f32[1,2,40,18,1]{2,1,4,3,0:T(2,128)S(1)}, u32[]{:S(2)}, u32[]{:S(2)}) collective-permute-start(f32[1,2,40,18,1]{2,1,4,3,0:T(2,128)S(1)} %copy.34), channel_id=1, source_target_pairs={{1,0},{0,1},{3,2},{2,3},{5,4},{4,5},{7,6},{6,7},{9,8},{8,9},{11,10... | collective-permute-start | bytes 17288 | tf_op jit(solution)/shard_map/while/body/eval_jaxpr/ppermute | solution.py:30
  90.2 6.7 %collective-permute-start = (f32[1,2,40,1,128]{4,2,3,1,0:T(8,128)S(1)}, f32[1,2,40,1,128]{4,2,3,1,0:T(8,128)S(1)}, u32[]{:S(2)}, u32[]{:S(2)}) collective-permute-start(f32[1,2,40,1,128]{4,2,3,1,0:T(8,128)S(1)} %get-tuple-element.102), channel_id=1, source_target_pairs={{0,2},{2,4},{4,6},{6,8},{8,10},{10,12},{12,14},{14,0},{1,3},{3,5},... | collective-permute-start | bytes 122888 | tf_op jit(solution)/shard_map/while/body/eval_jaxpr/ppermute | solution.py:28
  90.2 6.7 %collective-permute-start.1 = (f32[1,2,40,1,128]{4,2,3,1,0:T(8,128)S(1)}, f32[1,2,40,1,128]{4,2,3,1,0:T(8,128)S(1)}, u32[]{:S(2)}, u32[]{:S(2)}) collective-permute-start(f32[1,2,40,1,128]{4,2,3,1,0:T(8,128)S(1)} %get-tuple-element.103), channel_id=1, source_target_pairs={{2,0},{4,2},{6,4},{8,6},{10,8},{12,10},{14,12},{0,14},{3,1},{5,3},... | collective-permute-start | bytes 122888 | tf_op jit(solution)/shard_map/while/body/eval_jaxpr/ppermute | solution.py:30
  97.9 1.8 %collective-permute-start.3 = (f32[1,2,40,18,1]{2,1,4,3,0:T(2,128)S(1)}, f32[1,2,40,18,1]{2,1,4,3,0:T(2,128)S(1)}, u32[]{:S(2)}, u32[]{:S(2)}) collective-permute-start(f32[1,2,40,18,1]{2,1,4,3,0:T(2,128)S(1)} %copy.34), channel_id=1, source_target_pairs={{1,0},{0,1},{3,2},{2,3},{5,4},{4,5},{7,6},{6,7},{9,8},{8,9},{11,10... | collective-permute-start | bytes 17288 | tf_op jit(solution)/shard_map/while/body/eval_jaxpr/ppermute | solution.py:30
  102.5 6.7 %collective-permute-start = (f32[1,2,40,1,128]{4,2,3,1,0:T(8,128)S(1)}, f32[1,2,40,1,128]{4,2,3,1,0:T(8,128)S(1)}, u32[]{:S(2)}, u32[]{:S(2)}) collective-permute-start(f32[1,2,40,1,128]{4,2,3,1,0:T(8,128)S(1)} %get-tuple-element.102), channel_id=1, source_target_pairs={{0,2},{2,4},{4,6},{6,8},{8,10},{10,12},{12,14},{14,0},{1,3},{3,5},... | collective-permute-start | bytes 122888 | tf_op jit(solution)/shard_map/while/body/eval_jaxpr/ppermute | solution.py:28
  102.5 6.8 %collective-permute-start.1 = (f32[1,2,40,1,128]{4,2,3,1,0:T(8,128)S(1)}, f32[1,2,40,1,128]{4,2,3,1,0:T(8,128)S(1)}, u32[]{:S(2)}, u32[]{:S(2)}) collective-permute-start(f32[1,2,40,1,128]{4,2,3,1,0:T(8,128)S(1)} %get-tuple-element.103), channel_id=1, source_target_pairs={{2,0},{4,2},{6,4},{8,6},{10,8},{12,10},{14,12},{0,14},{3,1},{5,3},... | collective-permute-start | bytes 122888 | tf_op jit(solution)/shard_map/while/body/eval_jaxpr/ppermute | solution.py:30
  110.2 1.8 %collective-permute-start.3 = (f32[1,2,40,18,1]{2,1,4,3,0:T(2,128)S(1)}, f32[1,2,40,18,1]{2,1,4,3,0:T(2,128)S(1)}, u32[]{:S(2)}, u32[]{:S(2)}) collective-permute-start(f32[1,2,40,18,1]{2,1,4,3,0:T(2,128)S(1)} %copy.34), channel_id=1, source_target_pairs={{1,0},{0,1},{3,2},{2,3},{5,4},{4,5},{7,6},{6,7},{9,8},{8,9},{11,10... | collective-permute-start | bytes 17288 | tf_op jit(solution)/shard_map/while/body/eval_jaxpr/ppermute | solution.py:30
  114.8 6.7 %collective-permute-start = (f32[1,2,40,1,128]{4,2,3,1,0:T(8,128)S(1)}, f32[1,2,40,1,128]{4,2,3,1,0:T(8,128)S(1)}, u32[]{:S(2)}, u32[]{:S(2)}) collective-permute-start(f32[1,2,40,1,128]{4,2,3,1,0:T(8,128)S(1)} %get-tuple-element.102), channel_id=1, source_target_pairs={{0,2},{2,4},{4,6},{6,8},{8,10},{10,12},{12,14},{14,0},{1,3},{3,5},... | collective-permute-start | bytes 122888 | tf_op jit(solution)/shard_map/while/body/eval_jaxpr/ppermute | solution.py:28
  114.8 6.7 %collective-permute-start.1 = (f32[1,2,40,1,128]{4,2,3,1,0:T(8,128)S(1)}, f32[1,2,40,1,128]{4,2,3,1,0:T(8,128)S(1)}, u32[]{:S(2)}, u32[]{:S(2)}) collective-permute-start(f32[1,2,40,1,128]{4,2,3,1,0:T(8,128)S(1)} %get-tuple-element.103), channel_id=1, source_target_pairs={{2,0},{4,2},{6,4},{8,6},{10,8},{12,10},{14,12},{0,14},{3,1},{5,3},... | collective-permute-start | bytes 122888 | tf_op jit(solution)/shard_map/while/body/eval_jaxpr/ppermute | solution.py:30
  122.5 1.8 %collective-permute-start.3 = (f32[1,2,40,18,1]{2,1,4,3,0:T(2,128)S(1)}, f32[1,2,40,18,1]{2,1,4,3,0:T(2,128)S(1)}, u32[]{:S(2)}, u32[]{:S(2)}) collective-permute-start(f32[1,2,40,18,1]{2,1,4,3,0:T(2,128)S(1)} %copy.34), channel_id=1, source_target_pairs={{1,0},{0,1},{3,2},{2,3},{5,4},{4,5},{7,6},{6,7},{9,8},{8,9},{11,10... | collective-permute-start | bytes 17288 | tf_op jit(solution)/shard_map/while/body/eval_jaxpr/ppermute | solution.py:30
  127.1 6.7 %collective-permute-start = (f32[1,2,40,1,128]{4,2,3,1,0:T(8,128)S(1)}, f32[1,2,40,1,128]{4,2,3,1,0:T(8,128)S(1)}, u32[]{:S(2)}, u32[]{:S(2)}) collective-permute-start(f32[1,2,40,1,128]{4,2,3,1,0:T(8,128)S(1)} %get-tuple-element.102), channel_id=1, source_target_pairs={{0,2},{2,4},{4,6},{6,8},{8,10},{10,12},{12,14},{14,0},{1,3},{3,5},... | collective-permute-start | bytes 122888 | tf_op jit(solution)/shard_map/while/body/eval_jaxpr/ppermute | solution.py:28
  127.1 6.8 %collective-permute-start.1 = (f32[1,2,40,1,128]{4,2,3,1,0:T(8,128)S(1)}, f32[1,2,40,1,128]{4,2,3,1,0:T(8,128)S(1)}, u32[]{:S(2)}, u32[]{:S(2)}) collective-permute-start(f32[1,2,40,1,128]{4,2,3,1,0:T(8,128)S(1)} %get-tuple-element.103), channel_id=1, source_target_pairs={{2,0},{4,2},{6,4},{8,6},{10,8},{12,10},{14,12},{0,14},{3,1},{5,3},... | collective-permute-start | bytes 122888 | tf_op jit(solution)/shard_map/while/body/eval_jaxpr/ppermute | solution.py:30
  134.8 1.8 %collective-permute-start.3 = (f32[1,2,40,18,1]{2,1,4,3,0:T(2,128)S(1)}, f32[1,2,40,18,1]{2,1,4,3,0:T(2,128)S(1)}, u32[]{:S(2)}, u32[]{:S(2)}) collective-permute-start(f32[1,2,40,18,1]{2,1,4,3,0:T(2,128)S(1)} %copy.34), channel_id=1, source_target_pairs={{1,0},{0,1},{3,2},{2,3},{5,4},{4,5},{7,6},{6,7},{9,8},{8,9},{11,10... | collective-permute-start | bytes 17288 | tf_op jit(solution)/shard_map/while/body/eval_jaxpr/ppermute | solution.py:30
  139.4 6.7 %collective-permute-start = (f32[1,2,40,1,128]{4,2,3,1,0:T(8,128)S(1)}, f32[1,2,40,1,128]{4,2,3,1,0:T(8,128)S(1)}, u32[]{:S(2)}, u32[]{:S(2)}) collective-permute-start(f32[1,2,40,1,128]{4,2,3,1,0:T(8,128)S(1)} %get-tuple-element.102), channel_id=1, source_target_pairs={{0,2},{2,4},{4,6},{6,8},{8,10},{10,12},{12,14},{14,0},{1,3},{3,5},... | collective-permute-start | bytes 122888 | tf_op jit(solution)/shard_map/while/body/eval_jaxpr/ppermute | solution.py:28
  139.4 6.7 %collective-permute-start.1 = (f32[1,2,40,1,128]{4,2,3,1,0:T(8,128)S(1)}, f32[1,2,40,1,128]{4,2,3,1,0:T(8,128)S(1)}, u32[]{:S(2)}, u32[]{:S(2)}) collective-permute-start(f32[1,2,40,1,128]{4,2,3,1,0:T(8,128)S(1)} %get-tuple-element.103), channel_id=1, source_target_pairs={{2,0},{4,2},{6,4},{8,6},{10,8},{12,10},{14,12},{0,14},{3,1},{5,3},... | collective-permute-start | bytes 122888 | tf_op jit(solution)/shard_map/while/body/eval_jaxpr/ppermute | solution.py:30
  147.0 1.8 %collective-permute-start.3 = (f32[1,2,40,18,1]{2,1,4,3,0:T(2,128)S(1)}, f32[1,2,40,18,1]{2,1,4,3,0:T(2,128)S(1)}, u32[]{:S(2)}, u32[]{:S(2)}) collective-permute-start(f32[1,2,40,18,1]{2,1,4,3,0:T(2,128)S(1)} %copy.34), channel_id=1, source_target_pairs={{1,0},{0,1},{3,2},{2,3},{5,4},{4,5},{7,6},{6,7},{9,8},{8,9},{11,10... | collective-permute-start | bytes 17288 | tf_op jit(solution)/shard_map/while/body/eval_jaxpr/ppermute | solution.py:30
  151.7 6.7 %collective-permute-start = (f32[1,2,40,1,128]{4,2,3,1,0:T(8,128)S(1)}, f32[1,2,40,1,128]{4,2,3,1,0:T(8,128)S(1)}, u32[]{:S(2)}, u32[]{:S(2)}) collective-permute-start(f32[1,2,40,1,128]{4,2,3,1,0:T(8,128)S(1)} %get-tuple-element.102), channel_id=1, source_target_pairs={{0,2},{2,4},{4,6},{6,8},{8,10},{10,12},{12,14},{14,0},{1,3},{3,5},... | collective-permute-start | bytes 122888 | tf_op jit(solution)/shard_map/while/body/eval_jaxpr/ppermute | solution.py:28
  151.7 6.8 %collective-permute-start.1 = (f32[1,2,40,1,128]{4,2,3,1,0:T(8,128)S(1)}, f32[1,2,40,1,128]{4,2,3,1,0:T(8,128)S(1)}, u32[]{:S(2)}, u32[]{:S(2)}) collective-permute-start(f32[1,2,40,1,128]{4,2,3,1,0:T(8,128)S(1)} %get-tuple-element.103), channel_id=1, source_target_pairs={{2,0},{4,2},{6,4},{8,6},{10,8},{12,10},{14,12},{0,14},{3,1},{5,3},... | collective-permute-start | bytes 122888 | tf_op jit(solution)/shard_map/while/body/eval_jaxpr/ppermute | solution.py:30
  (13 other events, 47.7 us)
Sparse Core Ops, SparseCore 0:
  10.0 26.9 all-gather.1
where the time goes:
time: 172 us
  starting transfers between devices  57.3 us (33%)
  waiting for transfers between devices  49.7 us (29%)
  local copies, waits for them, and re-layouts  29.9 us (17%)
  other arithmetic  17.9 us (10%)
  between operations  13.4 us (8%)
  matrix products  3.01 us (2%)
    ppermute x20, starting transfers between devices, padded(): lax.ppermute(head, axis, [((i + 1) % count, i) for i in range(count)])  45.2 us
    ppermute x20, waiting for transfers between devices, padded(): lax.ppermute(tail, axis, [(i, (i + 1) % count) for i in range(count)])  27.5 us
    all_gather x1, waiting for transfers between devices, per_device(): lax.all_gather(masked, 'lev', axis=2, tiled=True)  19.4 us
    while x50, local copies, waits for them, and re-layouts  17.4 us
    mul x10, other arithmetic, relax(): return wet_center * (center + flux)  14.5 us
    ppermute x20, starting transfers between devices, padded(): lax.ppermute(tail, axis, [(i, (i + 1) % count) for i in range(count)])  7.65 us
  transfers between devices with their start and end apart: 43, of which 23 were waited for; matrix products, arithmetic and copies ran while one was open for 3% of the time, Pallas kernels for 0%

commit v1 on v0

--- a/solution.py
+++ b/solution.py
@@ -53,12 +53,25 @@
     wet_float = wet.astype(jnp.float32)
     masked = increments * wet_float
     own_rows = lax.dynamic_slice_in_dim(vert_corr, lev_first, lev_dev, 1)
-    correlated = jnp.einsum(
+    size, index = (lax.axis_size("lev"), lax.axis_index("lev"))
+    backward = [(i_2, (i_2 - 1) % size) for i_2 in range(size)]
+    rows = masked.shape[2]
+    held = masked
+    total = jnp.einsum(
         "toh,dthxy->dtoxy",
-        own_rows,
-        lax.all_gather(masked, "lev", axis=2, tiled=True),
+        lax.dynamic_slice_in_dim(own_rows, index * rows, held.shape[2], axis=2),
+        held,
         precision=lax.Precision.HIGHEST,
     )
+    for lap in range(1, size):
+        held = lax.ppermute(held, "lev", backward)
+        total = total + jnp.einsum(
+            "toh,dthxy->dtoxy",
+            lax.dynamic_slice_in_dim(own_rows, (index + lap) % size * rows, held.shape[2], axis=2),
+            held,
+            precision=lax.Precision.HIGHEST,
+        )
+    correlated = total
     field = correlated * wet_float
     total_y = cells_y * lax.axis_size("gy")
     local_rows = lax.axis_index("gy") * cells_y + jnp.arange(cells_y, dtype=jnp.int32)

time: 172 us -> 151 us (0.88)
  between operations: 13.4 us -> 0.1 us
  waiting for transfers between devices: 49.7 us -> 41 us
    all_gather x1 -> x0, waiting for transfers between devices: 19.4 us -> none  [per_device(): lax.all_gather(masked, 'lev', axis=2, tiled=True)]
    ppermute x0 -> x1, waiting for transfers between devices: none -> 13.4 us  [per_device(): held = lax.ppermute(held, 'lev', backward)]
    ppermute x1, waiting for transfers between devices: 2.12 us -> 0.01 us  [from_behind(): return lax.ppermute(block, axis, route)]
    mul x1, other arithmetic: 2.14 us -> 0.21 us  [per_device(): masked = increments * wet_float]
  transfers between devices with their start and end apart: 43 -> 43, of which waited for: 23 -> 21; matrix products, arithmetic and copies ran while one was open for 3% -> 5% of each run, Pallas kernels for 0% -> 0%
where the time goes in v1:
time: 151 us; the launch traced here: 150 us
  starting transfers between devices  58.8 us (39%)
  waiting for transfers between devices  41 us (27%)
  local copies, waits for them, and re-layouts  30.6 us (20%)
  other arithmetic  16.6 us (11%)
  matrix products  2.3 us (2%)
    ppermute x20, starting transfers between devices, padded(): lax.ppermute(head, axis, [((i + 1) % count, i) for i in range(count)])  45.2 us
    ppermute x20, waiting for transfers between devices, padded(): lax.ppermute(tail, axis, [(i, (i + 1) % count) for i in range(count)])  27.5 us
    while x50, local copies, waits for them, and re-layouts  17.4 us
    mul x10, other arithmetic, relax(): return wet_center * (center + flux)  14.4 us
    ppermute x1, waiting for transfers between devices, per_device(): held = lax.ppermute(held, 'lev', backward)  13.4 us
    ppermute x20, starting transfers between devices, padded(): lax.ppermute(tail, axis, [(i, (i + 1) % count) for i in range(count)])  7.68 us
    ppermute x10, local copies, waits for them, and re-layouts, padded(): lax.ppermute(head, axis, [((i + 1) % count, i) for i in range(count)])  3.31 us
    ppermute x10, local copies, waits for them, and re-layouts, padded(): lax.ppermute(tail, axis, [(i, (i + 1) % count) for i in range(count)])  3.3 us
  transfers between devices with their start and end apart: 43, of which 21 were waited for; matrix products, arithmetic and copies ran while one was open for 5% of the time, Pallas kernels for 0%

profile of v1, /device:TPU:0, one launch (start us, length us, event | category | flops | bytes accessed | tf_op | source)
XLA Modules:
  0.0 149.9 jit_solution(1145603845038606674)
XLA Ops:
  0.8 3.0 %collective-permute-start.5 = (f32[1,128]{1,0:T(1,128)S(1)}, f32[1,128]{1,0:T(1,128)S(1)}, u32[]{:S(2)}, u32[]{:S(2)}) collective-permute-start(f32[1,128]{1,0:T(1,128)S(1)} %slice_bitcast_fusion.1), channel_id=1, source_target_pairs={{14,0},{0,2},{2,4},{4,6},{6,8},{8,10},{10,12},{12,14},{15,1},{1,3}... | collective-permute-start | bytes 1544 | tf_op jit(solution)/shard_map/ppermute | solution.py:12
  4.5 1.4 collective-permute-start.6
  7.3 1.6 %collective-permute-start.4 = (f32[1,2,40,16,128]{4,2,3,1,0:T(8,128)S(1)}, f32[1,2,40,16,128]{4,2,3,1,0:T(8,128)S(1)}, u32[]{:S(2)}, u32[]{:S(2)}) collective-permute-start(f32[1,2,40,16,128]{4,2,3,1,0:T(8,128)S(1)} %copy_multiply_fusion), channel_id=1, source_target_pairs={{0,16},{16,0},{1,17},{17,1},{2,18},{18,2},{3,19},{19,3},{4,20},{20... | collective-permute-start | bytes 1966088 | tf_op jit(solution)/shard_map/ppermute | solution.py:67
  10.0 13.4 %collective-permute-done.4 = f32[1,2,40,16,128]{4,2,3,1,0:T(8,128)S(1)} collective-permute-done((f32[1,2,40,16,128]{4,2,3,1,0:T(8,128)S(1)}, f32[1,2,40,16,128]{4,2,3,1,0:T(8,128)S(1)}, u32[]{:S(2)}, u32[]{:S(2)}) %collective-permute-start.4) | collective-permute-done | bytes 655392 | tf_op jit(solution)/shard_map/ppermute | solution.py:67
  23.4 1.6 %fusion.14 = f32[1,2,40,16,128]{4,2,3,1,0:T(8,128)} fusion(f32[2,16,128,40]{2,3,1,0:T(8,128)S(1)} %fusion.16, f32[1,2,40,16,128]{4,2,3,1,0:T(8,128)S(1)} %collective-permute-done.4, f32[40,16,128]{2,0,1:T(8,128)S(1)} %fusion.18, f32[2,80,80]{2,1,0:T(8,128)S(1)} %copy-done, s32[]{:T(128)S(6)} %select_n.19, s32[]{:T(128)S(6)} %select_n.22), kind=kOutput, calls=%fused_computation.22 | convolution fusion | flops 78970880 | bytes 2334728 | tf_op jit(solution)/shard_map/toh,dthxy->dtoxy/dot_general | solution.py:68
  25.0 122.9 %while.10 = (s32[]{:T(128)}, f32[1,2,40,16,128]{4,2,3,1,0:T(8,128)}, f32[40,16,128]{2,0,1:T(8,128)S(1)}, f32[18,130]{1,0:T(8,128)S(1)}, f32[18,130]{1,0:T(8,128)S(1)}, /*index=5*/s32[]{:T(128)}) while((s32[]{:T(128)}, f32[1,2,40,16,128]{4,2,3,1,0:T(8,128)}, f32[40,16,128]{2,0,1:T(8,128)S(1)}, f32[18,130]{1,0:T(8,128)S(1)}, ...), condition=%wide.region_1.2_spmd, body=%wide.region_0.1_spmd.sunk | while | flops 2785282 | bytes 5959653 | solution.py:94
  26.1 1.5 %collective-permute-start = (f32[1,2,40,1,128]{4,2,3,1,0:T(8,128)S(1)}, f32[1,2,40,1,128]{4,2,3,1,0:T(8,128)S(1)}, u32[]{:S(2)}, u32[]{:S(2)}) collective-permute-start(f32[1,2,40,1,128]{4,2,3,1,0:T(8,128)S(1)} %get-tuple-element.102), channel_id=1, source_target_pairs={{0,2},{2,4},{4,6},{6,8},{8,10},{10,12},{12,14},{14,0},{1,3},{3,5},... | collective-permute-start | bytes 122888 | tf_op jit(solution)/shard_map/while/body/eval_jaxpr/ppermute | solution.py:28
  27.6 3.2 %collective-permute-start.1 = (f32[1,2,40,1,128]{4,2,3,1,0:T(8,128)S(1)}, f32[1,2,40,1,128]{4,2,3,1,0:T(8,128)S(1)}, u32[]{:S(2)}, u32[]{:S(2)}) collective-permute-start(f32[1,2,40,1,128]{4,2,3,1,0:T(8,128)S(1)} %get-tuple-element.103), channel_id=1, source_target_pairs={{2,0},{4,2},{6,4},{8,6},{10,8},{12,10},{14,12},{0,14},{3,1},{5,3},... | collective-permute-start | bytes 122888 | tf_op jit(solution)/shard_map/while/body/eval_jaxpr/ppermute | solution.py:30
  30.8 2.0 %collective-permute-done = f32[1,2,40,1,128]{4,2,3,1,0:T(8,128)S(1)} collective-permute-done((f32[1,2,40,1,128]{4,2,3,1,0:T(8,128)S(1)}, f32[1,2,40,1,128]{4,2,3,1,0:T(8,128)S(1)}, u32[]{:S(2)}, u32[]{:S(2)}) %collective-permute-start) | collective-permute-done | bytes 40992 | tf_op jit(solution)/shard_map/while/body/eval_jaxpr/ppermute | solution.py:28
  35.8 1.4 fusion.36
  39.5 3.6 %collective-permute-start.1 = (f32[1,2,40,1,128]{4,2,3,1,0:T(8,128)S(1)}, f32[1,2,40,1,128]{4,2,3,1,0:T(8,128)S(1)}, u32[]{:S(2)}, u32[]{:S(2)}) collective-permute-start(f32[1,2,40,1,128]{4,2,3,1,0:T(8,128)S(1)} %get-tuple-element.103), channel_id=1, source_target_pairs={{2,0},{4,2},{6,4},{8,6},{10,8},{12,10},{14,12},{0,14},{3,1},{5,3},... | collective-permute-start | bytes 122888 | tf_op jit(solution)/shard_map/while/body/eval_jaxpr/ppermute | solution.py:30
  43.1 2.0 %collective-permute-done = f32[1,2,40,1,128]{4,2,3,1,0:T(8,128)S(1)} collective-permute-done((f32[1,2,40,1,128]{4,2,3,1,0:T(8,128)S(1)}, f32[1,2,40,1,128]{4,2,3,1,0:T(8,128)S(1)}, u32[]{:S(2)}, u32[]{:S(2)}) %collective-permute-start) | collective-permute-done | bytes 40992 | tf_op jit(solution)/shard_map/while/body/eval_jaxpr/ppermute | solution.py:28
  48.1 1.4 fusion.36
  50.7 4.7 %collective-permute-start.1 = (f32[1,2,40,1,128]{4,2,3,1,0:T(8,128)S(1)}, f32[1,2,40,1,128]{4,2,3,1,0:T(8,128)S(1)}, u32[]{:S(2)}, u32[]{:S(2)}) collective-permute-start(f32[1,2,40,1,128]{4,2,3,1,0:T(8,128)S(1)} %get-tuple-element.103), channel_id=1, source_target_pairs={{2,0},{4,2},{6,4},{8,6},{10,8},{12,10},{14,12},{0,14},{3,1},{5,3},... | collective-permute-start | bytes 122888 | tf_op jit(solution)/shard_map/while/body/eval_jaxpr/ppermute | solution.py:30
  55.4 2.0 %collective-permute-done = f32[1,2,40,1,128]{4,2,3,1,0:T(8,128)S(1)} collective-permute-done((f32[1,2,40,1,128]{4,2,3,1,0:T(8,128)S(1)}, f32[1,2,40,1,128]{4,2,3,1,0:T(8,128)S(1)}, u32[]{:S(2)}, u32[]{:S(2)}) %collective-permute-start) | collective-permute-done | bytes 40992 | tf_op jit(solution)/shard_map/while/body/eval_jaxpr/ppermute | solution.py:28
  60.4 1.4 fusion.36
  62.9 4.7 %collective-permute-start.1 = (f32[1,2,40,1,128]{4,2,3,1,0:T(8,128)S(1)}, f32[1,2,40,1,128]{4,2,3,1,0:T(8,128)S(1)}, u32[]{:S(2)}, u32[]{:S(2)}) collective-permute-start(f32[1,2,40,1,128]{4,2,3,1,0:T(8,128)S(1)} %get-tuple-element.103), channel_id=1, source_target_pairs={{2,0},{4,2},{6,4},{8,6},{10,8},{12,10},{14,12},{0,14},{3,1},{5,3},... | collective-permute-start | bytes 122888 | tf_op jit(solution)/shard_map/while/body/eval_jaxpr/ppermute | solution.py:30
  67.6 2.0 %collective-permute-done = f32[1,2,40,1,128]{4,2,3,1,0:T(8,128)S(1)} collective-permute-done((f32[1,2,40,1,128]{4,2,3,1,0:T(8,128)S(1)}, f32[1,2,40,1,128]{4,2,3,1,0:T(8,128)S(1)}, u32[]{:S(2)}, u32[]{:S(2)}) %collective-permute-start) | collective-permute-done | bytes 40992 | tf_op jit(solution)/shard_map/while/body/eval_jaxpr/ppermute | solution.py:28
  72.7 1.4 fusion.36
  75.2 4.7 %collective-permute-start.1 = (f32[1,2,40,1,128]{4,2,3,1,0:T(8,128)S(1)}, f32[1,2,40,1,128]{4,2,3,1,0:T(8,128)S(1)}, u32[]{:S(2)}, u32[]{:S(2)}) collective-permute-start(f32[1,2,40,1,128]{4,2,3,1,0:T(8,128)S(1)} %get-tuple-element.103), channel_id=1, source_target_pairs={{2,0},{4,2},{6,4},{8,6},{10,8},{12,10},{14,12},{0,14},{3,1},{5,3},... | collective-permute-start | bytes 122888 | tf_op jit(solution)/shard_map/while/body/eval_jaxpr/ppermute | solution.py:30
  79.9 2.0 %collective-permute-done = f32[1,2,40,1,128]{4,2,3,1,0:T(8,128)S(1)} collective-permute-done((f32[1,2,40,1,128]{4,2,3,1,0:T(8,128)S(1)}, f32[1,2,40,1,128]{4,2,3,1,0:T(8,128)S(1)}, u32[]{:S(2)}, u32[]{:S(2)}) %collective-permute-start) | collective-permute-done | bytes 40992 | tf_op jit(solution)/shard_map/while/body/eval_jaxpr/ppermute | solution.py:28
  87.5 4.7 %collective-permute-start.1 = (f32[1,2,40,1,128]{4,2,3,1,0:T(8,128)S(1)}, f32[1,2,40,1,128]{4,2,3,1,0:T(8,128)S(1)}, u32[]{:S(2)}, u32[]{:S(2)}) collective-permute-start(f32[1,2,40,1,128]{4,2,3,1,0:T(8,128)S(1)} %get-tuple-element.103), channel_id=1, source_target_pairs={{2,0},{4,2},{6,4},{8,6},{10,8},{12,10},{14,12},{0,14},{3,1},{5,3},... | collective-permute-start | bytes 122888 | tf_op jit(solution)/shard_map/while/body/eval_jaxpr/ppermute | solution.py:30
  92.2 2.0 %collective-permute-done = f32[1,2,40,1,128]{4,2,3,1,0:T(8,128)S(1)} collective-permute-done((f32[1,2,40,1,128]{4,2,3,1,0:T(8,128)S(1)}, f32[1,2,40,1,128]{4,2,3,1,0:T(8,128)S(1)}, u32[]{:S(2)}, u32[]{:S(2)}) %collective-permute-start) | collective-permute-done | bytes 40992 | tf_op jit(solution)/shard_map/while/body/eval_jaxpr/ppermute | solution.py:28
  99.8 4.7 %collective-permute-start.1 = (f32[1,2,40,1,128]{4,2,3,1,0:T(8,128)S(1)}, f32[1,2,40,1,128]{4,2,3,1,0:T(8,128)S(1)}, u32[]{:S(2)}, u32[]{:S(2)}) collective-permute-start(f32[1,2,40,1,128]{4,2,3,1,0:T(8,128)S(1)} %get-tuple-element.103), channel_id=1, source_target_pairs={{2,0},{4,2},{6,4},{8,6},{10,8},{12,10},{14,12},{0,14},{3,1},{5,3},... | collective-permute-start | bytes 122888 | tf_op jit(solution)/shard_map/while/body/eval_jaxpr/ppermute | solution.py:30
  104.5 2.0 %collective-permute-done = f32[1,2,40,1,128]{4,2,3,1,0:T(8,128)S(1)} collective-permute-done((f32[1,2,40,1,128]{4,2,3,1,0:T(8,128)S(1)}, f32[1,2,40,1,128]{4,2,3,1,0:T(8,128)S(1)}, u32[]{:S(2)}, u32[]{:S(2)}) %collective-permute-start) | collective-permute-done | bytes 40992 | tf_op jit(solution)/shard_map/while/body/eval_jaxpr/ppermute | solution.py:28
  112.1 4.7 %collective-permute-start.1 = (f32[1,2,40,1,128]{4,2,3,1,0:T(8,128)S(1)}, f32[1,2,40,1,128]{4,2,3,1,0:T(8,128)S(1)}, u32[]{:S(2)}, u32[]{:S(2)}) collective-permute-start(f32[1,2,40,1,128]{4,2,3,1,0:T(8,128)S(1)} %get-tuple-element.103), channel_id=1, source_target_pairs={{2,0},{4,2},{6,4},{8,6},{10,8},{12,10},{14,12},{0,14},{3,1},{5,3},... | collective-permute-start | bytes 122888 | tf_op jit(solution)/shard_map/while/body/eval_jaxpr/ppermute | solution.py:30
  116.8 2.0 %collective-permute-done = f32[1,2,40,1,128]{4,2,3,1,0:T(8,128)S(1)} collective-permute-done((f32[1,2,40,1,128]{4,2,3,1,0:T(8,128)S(1)}, f32[1,2,40,1,128]{4,2,3,1,0:T(8,128)S(1)}, u32[]{:S(2)}, u32[]{:S(2)}) %collective-permute-start) | collective-permute-done | bytes 40992 | tf_op jit(solution)/shard_map/while/body/eval_jaxpr/ppermute | solution.py:28
  124.4 4.7 %collective-permute-start.1 = (f32[1,2,40,1,128]{4,2,3,1,0:T(8,128)S(1)}, f32[1,2,40,1,128]{4,2,3,1,0:T(8,128)S(1)}, u32[]{:S(2)}, u32[]{:S(2)}) collective-permute-start(f32[1,2,40,1,128]{4,2,3,1,0:T(8,128)S(1)} %get-tuple-element.103), channel_id=1, source_target_pairs={{2,0},{4,2},{6,4},{8,6},{10,8},{12,10},{14,12},{0,14},{3,1},{5,3},... | collective-permute-start | bytes 122888 | tf_op jit(solution)/shard_map/while/body/eval_jaxpr/ppermute | solution.py:30
  129.1 2.0 %collective-permute-done = f32[1,2,40,1,128]{4,2,3,1,0:T(8,128)S(1)} collective-permute-done((f32[1,2,40,1,128]{4,2,3,1,0:T(8,128)S(1)}, f32[1,2,40,1,128]{4,2,3,1,0:T(8,128)S(1)}, u32[]{:S(2)}, u32[]{:S(2)}) %collective-permute-start) | collective-permute-done | bytes 40992 | tf_op jit(solution)/shard_map/while/body/eval_jaxpr/ppermute | solution.py:28
  136.7 4.7 %collective-permute-start.1 = (f32[1,2,40,1,128]{4,2,3,1,0:T(8,128)S(1)}, f32[1,2,40,1,128]{4,2,3,1,0:T(8,128)S(1)}, u32[]{:S(2)}, u32[]{:S(2)}) collective-permute-start(f32[1,2,40,1,128]{4,2,3,1,0:T(8,128)S(1)} %get-tuple-element.103), channel_id=1, source_target_pairs={{2,0},{4,2},{6,4},{8,6},{10,8},{12,10},{14,12},{0,14},{3,1},{5,3},... | collective-permute-start | bytes 122888 | tf_op jit(solution)/shard_map/while/body/eval_jaxpr/ppermute | solution.py:30
  141.4 2.0 %collective-permute-done = f32[1,2,40,1,128]{4,2,3,1,0:T(8,128)S(1)} collective-permute-done((f32[1,2,40,1,128]{4,2,3,1,0:T(8,128)S(1)}, f32[1,2,40,1,128]{4,2,3,1,0:T(8,128)S(1)}, u32[]{:S(2)}, u32[]{:S(2)}) %collective-permute-start) | collective-permute-done | bytes 40992 | tf_op jit(solution)/shard_map/while/body/eval_jaxpr/ppermute | solution.py:28
  147.8 2.0 %copy.20 = f32[1,2,40,16,128]{4,3,2,1,0:T(8,128)} copy(f32[1,2,40,16,128]{4,2,3,1,0:T(8,128)} %get-tuple-element.32) | data formatting | bytes 1310720 | tf_op jit(solution)/shard_map/while | solution.py:94
  (198 shorter events, 54.7 us)
Async XLA Ops:
  0.8 9.1 %collective-permute-start.5 = (f32[1,128]{1,0:T(1,128)S(1)}, f32[1,128]{1,0:T(1,128)S(1)}, u32[]{:S(2)}, u32[]{:S(2)}) collective-permute-start(f32[1,128]{1,0:T(1,128)S(1)} %slice_bitcast_fusion.1), channel_id=1, source_target_pairs={{14,0},{0,2},{2,4},{4,6},{6,8},{8,10},{10,12},{12,14},{15,1},{1,3}... | collective-permute-start | bytes 1544 | tf_op jit(solution)/shard_map/ppermute | solution.py:12
  4.5 5.3 %collective-permute-start.6 = (f32[16,1]{1,0:T(8,128)S(1)}, f32[16,1]{1,0:T(8,128)S(1)}, u32[]{:S(2)}, u32[]{:S(2)}) collective-permute-start(f32[16,1]{1,0:T(8,128)S(1)} %slice.63), channel_id=1, source_target_pairs={{0,1},{2,3},{4,5},{6,7},{8,9},{10,11},{12,13},{14,15},{16,17},{18,... | collective-permute-start | bytes 200 | tf_op jit(solution)/shard_map/ppermute | solution.py:18
  7.3 16.1 %collective-permute-start.4 = (f32[1,2,40,16,128]{4,2,3,1,0:T(8,128)S(1)}, f32[1,2,40,16,128]{4,2,3,1,0:T(8,128)S(1)}, u32[]{:S(2)}, u32[]{:S(2)}) collective-permute-start(f32[1,2,40,16,128]{4,2,3,1,0:T(8,128)S(1)} %copy_multiply_fusion), channel_id=1, source_target_pairs={{0,16},{16,0},{1,17},{17,1},{2,18},{18,2},{3,19},{19,3},{4,20},{20... | collective-permute-start | bytes 1966088 | tf_op jit(solution)/shard_map/ppermute | solution.py:67
  26.1 6.7 %collective-permute-start = (f32[1,2,40,1,128]{4,2,3,1,0:T(8,128)S(1)}, f32[1,2,40,1,128]{4,2,3,1,0:T(8,128)S(1)}, u32[]{:S(2)}, u32[]{:S(2)}) collective-permute-start(f32[1,2,40,1,128]{4,2,3,1,0:T(8,128)S(1)} %get-tuple-element.102), channel_id=1, source_target_pairs={{0,2},{2,4},{4,6},{6,8},{8,10},{10,12},{12,14},{14,0},{1,3},{3,5},... | collective-permute-start | bytes 122888 | tf_op jit(solution)/shard_map/while/body/eval_jaxpr/ppermute | solution.py:28
  27.6 5.2 %collective-permute-start.1 = (f32[1,2,40,1,128]{4,2,3,1,0:T(8,128)S(1)}, f32[1,2,40,1,128]{4,2,3,1,0:T(8,128)S(1)}, u32[]{:S(2)}, u32[]{:S(2)}) collective-permute-start(f32[1,2,40,1,128]{4,2,3,1,0:T(8,128)S(1)} %get-tuple-element.103), channel_id=1, source_target_pairs={{2,0},{4,2},{6,4},{8,6},{10,8},{12,10},{14,12},{0,14},{3,1},{5,3},... | collective-permute-start | bytes 122888 | tf_op jit(solution)/shard_map/while/body/eval_jaxpr/ppermute | solution.py:30
  33.7 1.8 %collective-permute-start.3 = (f32[1,2,40,18,1]{2,1,4,3,0:T(2,128)S(1)}, f32[1,2,40,18,1]{2,1,4,3,0:T(2,128)S(1)}, u32[]{:S(2)}, u32[]{:S(2)}) collective-permute-start(f32[1,2,40,18,1]{2,1,4,3,0:T(2,128)S(1)} %copy.35), channel_id=1, source_target_pairs={{1,0},{0,1},{3,2},{2,3},{5,4},{4,5},{7,6},{6,7},{9,8},{8,9},{11,10... | collective-permute-start | bytes 17288 | tf_op jit(solution)/shard_map/while/body/eval_jaxpr/ppermute | solution.py:30
  38.4 6.7 %collective-permute-start = (f32[1,2,40,1,128]{4,2,3,1,0:T(8,128)S(1)}, f32[1,2,40,1,128]{4,2,3,1,0:T(8,128)S(1)}, u32[]{:S(2)}, u32[]{:S(2)}) collective-permute-start(f32[1,2,40,1,128]{4,2,3,1,0:T(8,128)S(1)} %get-tuple-element.102), channel_id=1, source_target_pairs={{0,2},{2,4},{4,6},{6,8},{8,10},{10,12},{12,14},{14,0},{1,3},{3,5},... | collective-permute-start | bytes 122888 | tf_op jit(solution)/shard_map/while/body/eval_jaxpr/ppermute | solution.py:28
  39.5 5.6 %collective-permute-start.1 = (f32[1,2,40,1,128]{4,2,3,1,0:T(8,128)S(1)}, f32[1,2,40,1,128]{4,2,3,1,0:T(8,128)S(1)}, u32[]{:S(2)}, u32[]{:S(2)}) collective-permute-start(f32[1,2,40,1,128]{4,2,3,1,0:T(8,128)S(1)} %get-tuple-element.103), channel_id=1, source_target_pairs={{2,0},{4,2},{6,4},{8,6},{10,8},{12,10},{14,12},{0,14},{3,1},{5,3},... | collective-permute-start | bytes 122888 | tf_op jit(solution)/shard_map/while/body/eval_jaxpr/ppermute | solution.py:30
  46.0 1.8 %collective-permute-start.3 = (f32[1,2,40,18,1]{2,1,4,3,0:T(2,128)S(1)}, f32[1,2,40,18,1]{2,1,4,3,0:T(2,128)S(1)}, u32[]{:S(2)}, u32[]{:S(2)}) collective-permute-start(f32[1,2,40,18,1]{2,1,4,3,0:T(2,128)S(1)} %copy.35), channel_id=1, source_target_pairs={{1,0},{0,1},{3,2},{2,3},{5,4},{4,5},{7,6},{6,7},{9,8},{8,9},{11,10... | collective-permute-start | bytes 17288 | tf_op jit(solution)/shard_map/while/body/eval_jaxpr/ppermute | solution.py:30
  50.6 6.7 %collective-permute-start = (f32[1,2,40,1,128]{4,2,3,1,0:T(8,128)S(1)}, f32[1,2,40,1,128]{4,2,3,1,0:T(8,128)S(1)}, u32[]{:S(2)}, u32[]{:S(2)}) collective-permute-start(f32[1,2,40,1,128]{4,2,3,1,0:T(8,128)S(1)} %get-tuple-element.102), channel_id=1, source_target_pairs={{0,2},{2,4},{4,6},{6,8},{8,10},{10,12},{12,14},{14,0},{1,3},{3,5},... | collective-permute-start | bytes 122888 | tf_op jit(solution)/shard_map/while/body/eval_jaxpr/ppermute | solution.py:28
  50.7 6.7 %collective-permute-start.1 = (f32[1,2,40,1,128]{4,2,3,1,0:T(8,128)S(1)}, f32[1,2,40,1,128]{4,2,3,1,0:T(8,128)S(1)}, u32[]{:S(2)}, u32[]{:S(2)}) collective-permute-start(f32[1,2,40,1,128]{4,2,3,1,0:T(8,128)S(1)} %get-tuple-element.103), channel_id=1, source_target_pairs={{2,0},{4,2},{6,4},{8,6},{10,8},{12,10},{14,12},{0,14},{3,1},{5,3},... | collective-permute-start | bytes 122888 | tf_op jit(solution)/shard_map/while/body/eval_jaxpr/ppermute | solution.py:30
  58.3 1.8 %collective-permute-start.3 = (f32[1,2,40,18,1]{2,1,4,3,0:T(2,128)S(1)}, f32[1,2,40,18,1]{2,1,4,3,0:T(2,128)S(1)}, u32[]{:S(2)}, u32[]{:S(2)}) collective-permute-start(f32[1,2,40,18,1]{2,1,4,3,0:T(2,128)S(1)} %copy.35), channel_id=1, source_target_pairs={{1,0},{0,1},{3,2},{2,3},{5,4},{4,5},{7,6},{6,7},{9,8},{8,9},{11,10... | collective-permute-start | bytes 17288 | tf_op jit(solution)/shard_map/while/body/eval_jaxpr/ppermute | solution.py:30
  62.9 6.7 %collective-permute-start = (f32[1,2,40,1,128]{4,2,3,1,0:T(8,128)S(1)}, f32[1,2,40,1,128]{4,2,3,1,0:T(8,128)S(1)}, u32[]{:S(2)}, u32[]{:S(2)}) collective-permute-start(f32[1,2,40,1,128]{4,2,3,1,0:T(8,128)S(1)} %get-tuple-element.102), channel_id=1, source_target_pairs={{0,2},{2,4},{4,6},{6,8},{8,10},{10,12},{12,14},{14,0},{1,3},{3,5},... | collective-permute-start | bytes 122888 | tf_op jit(solution)/shard_map/while/body/eval_jaxpr/ppermute | solution.py:28
  62.9 6.8 %collective-permute-start.1 = (f32[1,2,40,1,128]{4,2,3,1,0:T(8,128)S(1)}, f32[1,2,40,1,128]{4,2,3,1,0:T(8,128)S(1)}, u32[]{:S(2)}, u32[]{:S(2)}) collective-permute-start(f32[1,2,40,1,128]{4,2,3,1,0:T(8,128)S(1)} %get-tuple-element.103), channel_id=1, source_target_pairs={{2,0},{4,2},{6,4},{8,6},{10,8},{12,10},{14,12},{0,14},{3,1},{5,3},... | collective-permute-start | bytes 122888 | tf_op jit(solution)/shard_map/while/body/eval_jaxpr/ppermute | solution.py:30
  70.6 1.8 %collective-permute-start.3 = (f32[1,2,40,18,1]{2,1,4,3,0:T(2,128)S(1)}, f32[1,2,40,18,1]{2,1,4,3,0:T(2,128)S(1)}, u32[]{:S(2)}, u32[]{:S(2)}) collective-permute-start(f32[1,2,40,18,1]{2,1,4,3,0:T(2,128)S(1)} %copy.35), channel_id=1, source_target_pairs={{1,0},{0,1},{3,2},{2,3},{5,4},{4,5},{7,6},{6,7},{9,8},{8,9},{11,10... | collective-permute-start | bytes 17288 | tf_op jit(solution)/shard_map/while/body/eval_jaxpr/ppermute | solution.py:30
  75.2 6.7 %collective-permute-start = (f32[1,2,40,1,128]{4,2,3,1,0:T(8,128)S(1)}, f32[1,2,40,1,128]{4,2,3,1,0:T(8,128)S(1)}, u32[]{:S(2)}, u32[]{:S(2)}) collective-permute-start(f32[1,2,40,1,128]{4,2,3,1,0:T(8,128)S(1)} %get-tuple-element.102), channel_id=1, source_target_pairs={{0,2},{2,4},{4,6},{6,8},{8,10},{10,12},{12,14},{14,0},{1,3},{3,5},... | collective-permute-start | bytes 122888 | tf_op jit(solution)/shard_map/while/body/eval_jaxpr/ppermute | solution.py:28
  75.2 6.7 %collective-permute-start.1 = (f32[1,2,40,1,128]{4,2,3,1,0:T(8,128)S(1)}, f32[1,2,40,1,128]{4,2,3,1,0:T(8,128)S(1)}, u32[]{:S(2)}, u32[]{:S(2)}) collective-permute-start(f32[1,2,40,1,128]{4,2,3,1,0:T(8,128)S(1)} %get-tuple-element.103), channel_id=1, source_target_pairs={{2,0},{4,2},{6,4},{8,6},{10,8},{12,10},{14,12},{0,14},{3,1},{5,3},... | collective-permute-start | bytes 122888 | tf_op jit(solution)/shard_map/while/body/eval_jaxpr/ppermute | solution.py:30
  82.9 1.8 %collective-permute-start.3 = (f32[1,2,40,18,1]{2,1,4,3,0:T(2,128)S(1)}, f32[1,2,40,18,1]{2,1,4,3,0:T(2,128)S(1)}, u32[]{:S(2)}, u32[]{:S(2)}) collective-permute-start(f32[1,2,40,18,1]{2,1,4,3,0:T(2,128)S(1)} %copy.35), channel_id=1, source_target_pairs={{1,0},{0,1},{3,2},{2,3},{5,4},{4,5},{7,6},{6,7},{9,8},{8,9},{11,10... | collective-permute-start | bytes 17288 | tf_op jit(solution)/shard_map/while/body/eval_jaxpr/ppermute | solution.py:30
  87.5 6.7 %collective-permute-start = (f32[1,2,40,1,128]{4,2,3,1,0:T(8,128)S(1)}, f32[1,2,40,1,128]{4,2,3,1,0:T(8,128)S(1)}, u32[]{:S(2)}, u32[]{:S(2)}) collective-permute-start(f32[1,2,40,1,128]{4,2,3,1,0:T(8,128)S(1)} %get-tuple-element.102), channel_id=1, source_target_pairs={{0,2},{2,4},{4,6},{6,8},{8,10},{10,12},{12,14},{14,0},{1,3},{3,5},... | collective-permute-start | bytes 122888 | tf_op jit(solution)/shard_map/while/body/eval_jaxpr/ppermute | solution.py:28
  87.5 6.8 %collective-permute-start.1 = (f32[1,2,40,1,128]{4,2,3,1,0:T(8,128)S(1)}, f32[1,2,40,1,128]{4,2,3,1,0:T(8,128)S(1)}, u32[]{:S(2)}, u32[]{:S(2)}) collective-permute-start(f32[1,2,40,1,128]{4,2,3,1,0:T(8,128)S(1)} %get-tuple-element.103), channel_id=1, source_target_pairs={{2,0},{4,2},{6,4},{8,6},{10,8},{12,10},{14,12},{0,14},{3,1},{5,3},... | collective-permute-start | bytes 122888 | tf_op jit(solution)/shard_map/while/body/eval_jaxpr/ppermute | solution.py:30
  95.2 1.8 %collective-permute-start.3 = (f32[1,2,40,18,1]{2,1,4,3,0:T(2,128)S(1)}, f32[1,2,40,18,1]{2,1,4,3,0:T(2,128)S(1)}, u32[]{:S(2)}, u32[]{:S(2)}) collective-permute-start(f32[1,2,40,18,1]{2,1,4,3,0:T(2,128)S(1)} %copy.35), channel_id=1, source_target_pairs={{1,0},{0,1},{3,2},{2,3},{5,4},{4,5},{7,6},{6,7},{9,8},{8,9},{11,10... | collective-permute-start | bytes 17288 | tf_op jit(solution)/shard_map/while/body/eval_jaxpr/ppermute | solution.py:30
  99.8 6.7 %collective-permute-start = (f32[1,2,40,1,128]{4,2,3,1,0:T(8,128)S(1)}, f32[1,2,40,1,128]{4,2,3,1,0:T(8,128)S(1)}, u32[]{:S(2)}, u32[]{:S(2)}) collective-permute-start(f32[1,2,40,1,128]{4,2,3,1,0:T(8,128)S(1)} %get-tuple-element.102), channel_id=1, source_target_pairs={{0,2},{2,4},{4,6},{6,8},{8,10},{10,12},{12,14},{14,0},{1,3},{3,5},... | collective-permute-start | bytes 122888 | tf_op jit(solution)/shard_map/while/body/eval_jaxpr/ppermute | solution.py:28
  99.8 6.7 %collective-permute-start.1 = (f32[1,2,40,1,128]{4,2,3,1,0:T(8,128)S(1)}, f32[1,2,40,1,128]{4,2,3,1,0:T(8,128)S(1)}, u32[]{:S(2)}, u32[]{:S(2)}) collective-permute-start(f32[1,2,40,1,128]{4,2,3,1,0:T(8,128)S(1)} %get-tuple-element.103), channel_id=1, source_target_pairs={{2,0},{4,2},{6,4},{8,6},{10,8},{12,10},{14,12},{0,14},{3,1},{5,3},... | collective-permute-start | bytes 122888 | tf_op jit(solution)/shard_map/while/body/eval_jaxpr/ppermute | solution.py:30
  107.4 1.8 %collective-permute-start.3 = (f32[1,2,40,18,1]{2,1,4,3,0:T(2,128)S(1)}, f32[1,2,40,18,1]{2,1,4,3,0:T(2,128)S(1)}, u32[]{:S(2)}, u32[]{:S(2)}) collective-permute-start(f32[1,2,40,18,1]{2,1,4,3,0:T(2,128)S(1)} %copy.35), channel_id=1, source_target_pairs={{1,0},{0,1},{3,2},{2,3},{5,4},{4,5},{7,6},{6,7},{9,8},{8,9},{11,10... | collective-permute-start | bytes 17288 | tf_op jit(solution)/shard_map/while/body/eval_jaxpr/ppermute | solution.py:30
  112.1 6.7 %collective-permute-start = (f32[1,2,40,1,128]{4,2,3,1,0:T(8,128)S(1)}, f32[1,2,40,1,128]{4,2,3,1,0:T(8,128)S(1)}, u32[]{:S(2)}, u32[]{:S(2)}) collective-permute-start(f32[1,2,40,1,128]{4,2,3,1,0:T(8,128)S(1)} %get-tuple-element.102), channel_id=1, source_target_pairs={{0,2},{2,4},{4,6},{6,8},{8,10},{10,12},{12,14},{14,0},{1,3},{3,5},... | collective-permute-start | bytes 122888 | tf_op jit(solution)/shard_map/while/body/eval_jaxpr/ppermute | solution.py:28
  112.1 6.8 %collective-permute-start.1 = (f32[1,2,40,1,128]{4,2,3,1,0:T(8,128)S(1)}, f32[1,2,40,1,128]{4,2,3,1,0:T(8,128)S(1)}, u32[]{:S(2)}, u32[]{:S(2)}) collective-permute-start(f32[1,2,40,1,128]{4,2,3,1,0:T(8,128)S(1)} %get-tuple-element.103), channel_id=1, source_target_pairs={{2,0},{4,2},{6,4},{8,6},{10,8},{12,10},{14,12},{0,14},{3,1},{5,3},... | collective-permute-start | bytes 122888 | tf_op jit(solution)/shard_map/while/body/eval_jaxpr/ppermute | solution.py:30
  119.7 1.8 %collective-permute-start.3 = (f32[1,2,40,18,1]{2,1,4,3,0:T(2,128)S(1)}, f32[1,2,40,18,1]{2,1,4,3,0:T(2,128)S(1)}, u32[]{:S(2)}, u32[]{:S(2)}) collective-permute-start(f32[1,2,40,18,1]{2,1,4,3,0:T(2,128)S(1)} %copy.35), channel_id=1, source_target_pairs={{1,0},{0,1},{3,2},{2,3},{5,4},{4,5},{7,6},{6,7},{9,8},{8,9},{11,10... | collective-permute-start | bytes 17288 | tf_op jit(solution)/shard_map/while/body/eval_jaxpr/ppermute | solution.py:30
  124.4 6.7 %collective-permute-start = (f32[1,2,40,1,128]{4,2,3,1,0:T(8,128)S(1)}, f32[1,2,40,1,128]{4,2,3,1,0:T(8,128)S(1)}, u32[]{:S(2)}, u32[]{:S(2)}) collective-permute-start(f32[1,2,40,1,128]{4,2,3,1,0:T(8,128)S(1)} %get-tuple-element.102), channel_id=1, source_target_pairs={{0,2},{2,4},{4,6},{6,8},{8,10},{10,12},{12,14},{14,0},{1,3},{3,5},... | collective-permute-start | bytes 122888 | tf_op jit(solution)/shard_map/while/body/eval_jaxpr/ppermute | solution.py:28
  124.4 6.7 %collective-permute-start.1 = (f32[1,2,40,1,128]{4,2,3,1,0:T(8,128)S(1)}, f32[1,2,40,1,128]{4,2,3,1,0:T(8,128)S(1)}, u32[]{:S(2)}, u32[]{:S(2)}) collective-permute-start(f32[1,2,40,1,128]{4,2,3,1,0:T(8,128)S(1)} %get-tuple-element.103), channel_id=1, source_target_pairs={{2,0},{4,2},{6,4},{8,6},{10,8},{12,10},{14,12},{0,14},{3,1},{5,3},... | collective-permute-start | bytes 122888 | tf_op jit(solution)/shard_map/while/body/eval_jaxpr/ppermute | solution.py:30
  132.0 1.8 %collective-permute-start.3 = (f32[1,2,40,18,1]{2,1,4,3,0:T(2,128)S(1)}, f32[1,2,40,18,1]{2,1,4,3,0:T(2,128)S(1)}, u32[]{:S(2)}, u32[]{:S(2)}) collective-permute-start(f32[1,2,40,18,1]{2,1,4,3,0:T(2,128)S(1)} %copy.35), channel_id=1, source_target_pairs={{1,0},{0,1},{3,2},{2,3},{5,4},{4,5},{7,6},{6,7},{9,8},{8,9},{11,10... | collective-permute-start | bytes 17288 | tf_op jit(solution)/shard_map/while/body/eval_jaxpr/ppermute | solution.py:30
  136.6 6.7 %collective-permute-start = (f32[1,2,40,1,128]{4,2,3,1,0:T(8,128)S(1)}, f32[1,2,40,1,128]{4,2,3,1,0:T(8,128)S(1)}, u32[]{:S(2)}, u32[]{:S(2)}) collective-permute-start(f32[1,2,40,1,128]{4,2,3,1,0:T(8,128)S(1)} %get-tuple-element.102), channel_id=1, source_target_pairs={{0,2},{2,4},{4,6},{6,8},{8,10},{10,12},{12,14},{14,0},{1,3},{3,5},... | collective-permute-start | bytes 122888 | tf_op jit(solution)/shard_map/while/body/eval_jaxpr/ppermute | solution.py:28
  136.7 6.8 %collective-permute-start.1 = (f32[1,2,40,1,128]{4,2,3,1,0:T(8,128)S(1)}, f32[1,2,40,1,128]{4,2,3,1,0:T(8,128)S(1)}, u32[]{:S(2)}, u32[]{:S(2)}) collective-permute-start(f32[1,2,40,1,128]{4,2,3,1,0:T(8,128)S(1)} %get-tuple-element.103), channel_id=1, source_target_pairs={{2,0},{4,2},{6,4},{8,6},{10,8},{12,10},{14,12},{0,14},{3,1},{5,3},... | collective-permute-start | bytes 122888 | tf_op jit(solution)/shard_map/while/body/eval_jaxpr/ppermute | solution.py:30
  (14 other events, 32.0 us)
